TPU v7x, 512 devices: a whole 4x8x8 slice. The times are simulated.
512 devices in a mesh: section: 32 (over z_lo, y), tensor: 16 (over x, z_hi, core).
Axes of the slice: x: 4, y: 8, z: 8 (z_hi: 2, z_lo: 4; z = z_hi * 4 + z_lo), core: 2. Of those that a mesh axis runs over, the one named last changes fastest.
Arguments:
- vision_tokens: bfloat16 [2048, 1664], P('section'), may hold values from -6 to 6
- key_weight: bfloat16 [13312, 8192], P('section', 'tensor'), may hold values from -0.15625 to 0.15625
- value_weight: bfloat16 [13312, 8192], P('section', 'tensor'), may hold values from -0.15625 to 0.15625
- queries: bfloat16 [32, 1024, 8192], P('section', None, 'tensor'), may hold values from -6 to 6
- gate: float32 [8], replicated, may hold values from 0.3 to 1.5
- visible: int32 [4, 4, 4], replicated, may hold values from -1 to 1, as said below
- out_grad: bfloat16 [32, 1024, 8192], P('section', None, 'tensor'), may hold values from -6 to 6
Outputs:
- attended: bfloat16 [32, 1024, 8192], P('section', None, 'tensor')
- vision_grad: bfloat16 [2048, 1664], P('section')
Inputs may be any that keep to these rules, and one draw needn't show every extreme that they name: `visible`: each row of 4 entries is non-decreasing, and every image index 0 to 1 occurs in every row.
All inputs are finite; a program needn't handle non-finite values.
Results may differ from a plain program's by a relative error of at most 0.029.
Values may be sent and summed in bfloat16 or wider, within the bound.
A program may use at most 64 MiB of HBM per device.

v0:
```python
import jax
import jax.numpy as jnp
from jax import lax
from jax.sharding import PartitionSpec as P

HD = 128
IMG_TOK = 64
TBLOCK = 64
IMGS = 2
MICRO = 4


def from_partner(value, axis, distance):
    mask = 2**distance
    pairs = [(source, source ^ mask) for source in range(lax.axis_size(axis))]
    return lax.ppermute(value, axis, pairs)


def block_index(visible):
    samples = visible.shape[0]
    base = jnp.arange(samples, dtype=jnp.int32)[:, None] * IMGS
    seen = (base + jnp.maximum(visible, 0)).reshape(-1)
    validf = (visible >= 0).reshape(-1).astype(jnp.float32)
    return (seen, validf)


def local_layer(key_rows, value_rows, query, gate_value, cotangent, visible, heads):
    width = heads * HD
    seen, validf = block_index(visible)
    images = key_rows.shape[0] // IMG_TOK
    key_img = jnp.take(key_rows.reshape(images, IMG_TOK, heads, HD), seen, axis=0)
    val_img = jnp.take(value_rows.reshape(images, IMG_TOK, heads, HD), seen, axis=0)
    blocks = seen.shape[0]
    query_b = query.reshape(blocks, TBLOCK, heads, HD)
    scale = 1.0 / HD**0.5
    scores = (
        jnp.einsum("bqhd,bkhd->bhqk", query_b, key_img, preferred_element_type=jnp.float32) * scale
    )
    exponent = jnp.exp(scores)
    probs = exponent / jnp.sum(exponent, axis=-1, keepdims=True) * validf[:, None, None, None]
    probs_b = probs.astype(jnp.bfloat16)
    mixed = jnp.einsum("bhqk,bkhd->bqhd", probs_b, val_img, preferred_element_type=jnp.float32)
    factor = jnp.tanh(gate_value)
    attended = (factor * mixed).astype(jnp.bfloat16).reshape(-1, width)
    head_grad = (
        (factor * cotangent.astype(jnp.float32))
        .astype(jnp.bfloat16)
        .reshape(blocks, TBLOCK, heads, HD)
    )
    vgrad_blk = jnp.einsum(
        "bhqk,bqhd->bkhd", probs_b, head_grad, preferred_element_type=jnp.float32
    )
    prob_grad = jnp.einsum(
        "bqhd,bkhd->bhqk", head_grad, val_img, preferred_element_type=jnp.float32
    )
    delta = jnp.sum(probs * prob_grad, axis=-1, keepdims=True)
    score_grad = (probs * (prob_grad - delta) * scale).astype(jnp.bfloat16)
    kgrad_blk = jnp.einsum(
        "bhqk,bqhd->bkhd", score_grad, query_b, preferred_element_type=jnp.float32
    )
    onehot = (seen[:, None] == jnp.arange(images, dtype=jnp.int32)[None, :]).astype(jnp.float32)
    key_grad = (
        jnp.einsum("bi,bkhd->ikhd", onehot, kgrad_blk).reshape(-1, width).astype(jnp.bfloat16)
    )
    value_grad = (
        jnp.einsum("bi,bkhd->ikhd", onehot, vgrad_blk).reshape(-1, width).astype(jnp.bfloat16)
    )
    return (attended, key_grad, value_grad)


def back_product(grad_rows, weight):
    return lax.dot_general(
        grad_rows, weight, (((1,), (1,)), ((), ())), preferred_element_type=jnp.float32
    )


def upper_bit(position, bit):
    return position // 2**bit % 2 == 1


def join_pair(mine, partner, upper, axis):
    low_first = jnp.concatenate([mine, partner], axis=axis)
    high_first = jnp.concatenate([partner, mine], axis=axis)
    return jnp.where(upper, high_first, low_first)


def split_pair(values, upper):
    half = values.shape[0] // 2
    lower_rows = values[:half]
    upper_rows = values[half:]
    keep = jnp.where(upper, upper_rows, lower_rows)
    give = jnp.where(upper, lower_rows, upper_rows)
    return (keep, give)


def reduce_first(values, position, layer_bits):
    for bit in reversed(range(layer_bits)):
        keep, give = split_pair(values, upper_bit(position, bit))
        values = keep + from_partner(give.astype(jnp.bfloat16), "section", bit).astype(give.dtype)
    return values


def shards(vision_tokens, key_weight, value_weight, queries, gate, visible, out_grad):
    position = lax.axis_index("section")
    layers = lax.axis_size("section") // MICRO
    layer_bits = layers.bit_length() - 1
    layer = position % layers
    micro = position // layers
    stacked = jnp.stack([key_weight, value_weight])
    for offset in range(2):
        bit = layer_bits + offset
        partner = from_partner(stacked, "section", bit)
        stacked = join_pair(stacked, partner, upper_bit(position, bit), 1)
    w_key = stacked[0]
    w_value = stacked[1]
    width = w_key.shape[1]
    heads = width // HD
    gate_value = lax.dynamic_index_in_dim(gate, layer, 0, keepdims=False)
    own_visible = lax.dynamic_index_in_dim(visible, micro, 0, keepdims=False)
    all_rows = vision_tokens
    for bit in range(layer_bits):
        partner = from_partner(all_rows, "section", bit)
        all_rows = join_pair(all_rows, partner, upper_bit(position, bit), 0)
    key_rows = jnp.dot(all_rows, w_key, preferred_element_type=jnp.float32).astype(jnp.bfloat16)
    value_rows = jnp.dot(all_rows, w_value, preferred_element_type=jnp.float32).astype(jnp.bfloat16)
    attended, key_grad, value_grad = local_layer(
        key_rows, value_rows, queries[0], gate_value, out_grad[0], own_visible, heads
    )
    term = back_product(key_grad, w_key) + back_product(value_grad, w_value)
    summed = lax.psum(term.astype(jnp.bfloat16), "tensor").astype(jnp.float32)
    owned = reduce_first(summed, position, layer_bits).astype(jnp.bfloat16)
    return (attended[None], owned)


def solution(mesh):
    placed = (
        P("section", None),
        P("section", "tensor"),
        P("section", "tensor"),
        P("section", None, "tensor"),
        P(),
        P(),
        P("section", None, "tensor"),
    )
    return jax.shard_map(
        shards,
        mesh=mesh,
        in_specs=placed,
        out_specs=(P("section", None, "tensor"), P("section", None)),
        check_vma=False,
    )
```

profile of v0, /device:TPU:1, one launch (start us, length us, event | category | flops | bytes accessed | tf_op | source)
XLA Modules:
  0.0 440.8 jit_solution(11001433239776774613)
XLA Ops:
  7.2 1.2 pad_maximum_fusion
  8.5 5.0 %collective-permute-start.3 = (bf16[2,416,512]{2,1,0:T(8,128)(2,1)S(1)}, bf16[2,416,512]{2,1,0:T(8,128)(2,1)S(1)}, u32[]{:S(2)}, u32[]{:S(2)}) collective-permute-start(bf16[2,416,512]{2,1,0:T(8,128)(2,1)S(1)} %pad_maximum_fusion), channel_id=1, source_target_pairs={{0,128},{16,144},{32,160},{48,176},{64,192},{80,208},{96,224},{112... | collective-permute-start | bytes 2555912 | tf_op jit(solution)/shard_map/ppermute | solution.py:16
  13.5 14.5 %collective-permute-done.3 = bf16[2,416,512]{2,1,0:T(8,128)(2,1)S(1)} collective-permute-done((bf16[2,416,512]{2,1,0:T(8,128)(2,1)S(1)}, bf16[2,416,512]{2,1,0:T(8,128)(2,1)S(1)}, u32[]{:S(2)}, u32[]{:S(2)}) %collective-permute-start.3) | collective-permute-done | bytes 852000 | tf_op jit(solution)/shard_map/ppermute | solution.py:16
  28.0 2.0 maximum_select_fusion.2
  30.0 9.9 %collective-permute-start.4 = (bf16[2,832,512]{2,1,0:T(8,128)(2,1)S(1)}, bf16[2,832,512]{2,1,0:T(8,128)(2,1)}, u32[]{:S(2)}, u32[]{:S(2)}) collective-permute-start(bf16[2,832,512]{2,1,0:T(8,128)(2,1)S(1)} %maximum_select_fusion.2), channel_id=1, source_target_pairs={{0,256},{16,272},{32,288},{48,304},{64,320},{80,336},{96,352},{112... | collective-permute-start | bytes 5111816 | tf_op jit(solution)/shard_map/ppermute | solution.py:16
  39.9 3.2 collective-permute-start
  43.3 0.6 dynamic_slice.8
  44.8 2.3 collective-permute-done
  47.1 4.2 collective-permute-start.1
  51.4 1.4 multiply_convert_fusion.1
  52.8 16.9 %collective-permute-done.1 = bf16[128,1664]{1,0:T(8,128)(2,1)S(1)} collective-permute-done((bf16[128,1664]{1,0:T(8,128)(2,1)S(1)}, bf16[128,1664]{1,0:T(8,128)(2,1)S(1)}, u32[]{:S(2)}, u32[]{:S(2)}) %collective-permute-start.1) | collective-permute-done | bytes 426016 | tf_op jit(solution)/shard_map/ppermute | solution.py:16
  69.7 1.1 maximum_select_fusion.3
  70.8 8.4 %collective-permute-start.2 = (bf16[256,1664]{1,0:T(8,128)(2,1)}, bf16[256,1664]{1,0:T(8,128)(2,1)}, u32[]{:S(2)}, u32[]{:S(2)}) collective-permute-start(bf16[256,1664]{1,0:T(8,128)(2,1)} %maximum_select_fusion.3), channel_id=1, source_target_pairs={{0,64},{16,80},{32,96},{48,112},{64,0},{80,16},{96,32},{112,48},{1... | collective-permute-start | bytes 2555912 | tf_op jit(solution)/shard_map/ppermute | solution.py:16
  79.3 2.1 reshape_squeeze.3
  81.4 1.1 convert_element_type.89
  82.6 30.7 %collective-permute-done.4 = bf16[2,832,512]{2,1,0:T(8,128)(2,1)} collective-permute-done((bf16[2,832,512]{2,1,0:T(8,128)(2,1)S(1)}, bf16[2,832,512]{2,1,0:T(8,128)(2,1)}, u32[]{:S(2)}, u32[]{:S(2)}) %collective-permute-start.4) | collective-permute-done | bytes 1703968 | tf_op jit(solution)/shard_map/ppermute | solution.py:16
  113.3 3.9 maximum_select_fusion
  117.2 3.9 fusion.19
  121.1 2.0 reshape.62
  123.1 2.0 copy.13
  125.0 3.9 fusion.18
  128.9 2.0 reshape.63
  130.9 2.0 copy.14
  132.9 2.7 gather_fusion
  135.6 2.7 gather_fusion.1
  138.3 2.5 bitcast_reduce_fusion
  140.8 2.1 fusion.32
  142.8 1.7 fusion.30
  144.5 6.1 %fusion.12 = bf16[16,4,64,128]{3,2,1,0:T(8,128)(2,1)} fusion(f32[16,4,64,64]{2,3,1,0:T(8,128)} %fusion.32, bf16[16,64,4,128]{3,2,1,0:T(4,128)(2,1)} %reshape_squeeze.3, f32[16,4,64,64]{3,2,1,0:T(8,128)} %copy-done.7, f32[16]{0:T(128)S(1)} %reshape.64, f32[16,4,64]{2,1,0:T(4,128)S(1)} %get-tuple-element.5), kind=kOutput, calls=%fused_computation.20 | convolution fusion | flops 69996608 | bytes 4210752 | tf_op jit(solution)/shard_map/bhqk,bqhd->bkhd/dot_general | solution.py:58
  150.6 2.0 fusion.23
  152.6 2.0 fusion.20
  154.5 0.2 copy.20
  154.7 0.2 copy.21
  155.0 1.2 fusion.14
  156.1 2.4 add_convert_fusion
  158.5 196.9 %all-reduce.2.cloned.1.call-done = bf16[512,1664]{1,0:T(8,128)(2,1)} async-done(((bf16[512,1664]{1,0:T(8,128)(2,1)}), bf16[512,1664]{1,0:T(8,128)(2,1)}) %all-reduce.2.cloned.1.call-update) | async-done | bytes 1703952 | tf_op jit(solution)/shard_map/psum | solution.py:130
  355.4 1.7 convert_element_type.96
  357.3 7.2 %collective-permute-start.5 = (bf16[256,1664]{1,0:T(8,128)(2,1)S(1)}, bf16[256,1664]{1,0:T(8,128)(2,1)S(1)}, u32[]{:S(2)}, u32[]{:S(2)}) collective-permute-start(bf16[256,1664]{1,0:T(8,128)(2,1)S(1)} %select_convert_fusion), channel_id=1, source_target_pairs={{0,64},{16,80},{32,96},{48,112},{64,0},{80,16},{96,32},{112,48},{1... | collective-permute-start | bytes 2555912 | tf_op jit(solution)/shard_map/ppermute | solution.py:16
  364.5 29.0 %collective-permute-done.5 = bf16[256,1664]{1,0:T(8,128)(2,1)S(1)} collective-permute-done((bf16[256,1664]{1,0:T(8,128)(2,1)S(1)}, bf16[256,1664]{1,0:T(8,128)(2,1)S(1)}, u32[]{:S(2)}, u32[]{:S(2)}) %collective-permute-start.5) | collective-permute-done | bytes 852000 | tf_op jit(solution)/shard_map/ppermute | solution.py:16
  393.5 0.2 convert_add_fusion
  393.8 13.0 %collective-permute-start.6 = (bf16[128,1664]{1,0:T(8,128)(2,1)S(1)}, bf16[128,1664]{1,0:T(8,128)(2,1)S(1)}, u32[]{:S(2)}, u32[]{:S(2)}) collective-permute-start(bf16[128,1664]{1,0:T(8,128)(2,1)S(1)} %select_convert_fusion.1), channel_id=1, source_target_pairs={{0,32},{16,48},{32,0},{48,16},{64,96},{80,112},{96,64},{112,80},{1... | collective-permute-start | bytes 1277960 | tf_op jit(solution)/shard_map/ppermute | solution.py:16
  406.8 18.7 %collective-permute-done.6 = bf16[128,1664]{1,0:T(8,128)(2,1)S(1)} collective-permute-done((bf16[128,1664]{1,0:T(8,128)(2,1)S(1)}, bf16[128,1664]{1,0:T(8,128)(2,1)S(1)}, u32[]{:S(2)}, u32[]{:S(2)}) %collective-permute-start.6) | collective-permute-done | bytes 426016 | tf_op jit(solution)/shard_map/ppermute | solution.py:16
  425.7 1.9 collective-permute-start.7
  427.7 0.9 fusion.17
  428.6 0.9 copy.18
  429.5 1.2 broadcast_in_dim_reshape.4
  430.7 2.6 collective-permute-done.7
  433.2 0.7 add_convert_fusion.1
  (36 shorter events, 0.9 us)
Async XLA Ops:
  7.2 348.3 %all-reduce.2.cloned.1.call-start = ((), (), s32[]{:S(2)}) async-start(), calls=%async_computation | async-start | bytes 3407872 | tf_op jit(solution)/shard_map/psum | solution.py:130
  8.4 31.5 %copy-start.4 = (bf16[64,1664]{1,0:T(8,128)(2,1)S(1)}, bf16[64,1664]{1,0:T(8,128)(2,1)}, u32[]{:S(2)}) copy-start(bf16[64,1664]{1,0:T(8,128)(2,1)} %param.9) | copy-start | bytes 638980
  8.4 34.8 %copy-start.6 = (f32[8]{0:T(128)S(1)}, f32[8]{0:T(128)}, u32[]{:S(2)}) copy-start(f32[8]{0:T(128)} %param.13) | copy-start | bytes 100
  8.5 36.2 %copy-start.5 = (s32[4,4,4]{2,1,0:T(4,128)S(1)}, s32[4,4,4]{2,1,0:T(4,128)}, u32[]{:S(2)}) copy-start(s32[4,4,4]{2,1,0:T(4,128)} %param.14) | copy-start | bytes 772
  8.5 19.5 %collective-permute-start.3 = (bf16[2,416,512]{2,1,0:T(8,128)(2,1)S(1)}, bf16[2,416,512]{2,1,0:T(8,128)(2,1)S(1)}, u32[]{:S(2)}, u32[]{:S(2)}) collective-permute-start(bf16[2,416,512]{2,1,0:T(8,128)(2,1)S(1)} %pad_maximum_fusion), channel_id=1, source_target_pairs={{0,128},{16,144},{32,160},{48,176},{64,192},{80,208},{96,224},{112... | collective-permute-start | bytes 2555912 | tf_op jit(solution)/shard_map/ppermute | solution.py:16
  29.9 40.8 %copy-start = (bf16[2,832,512]{2,1,0:T(8,128)(2,1)}, bf16[2,832,512]{2,1,0:T(8,128)(2,1)S(1)}, u32[]{:S(2)}) copy-start(bf16[2,832,512]{2,1,0:T(8,128)(2,1)S(1)} %maximum_select_fusion.2) | copy-start | bytes 5111812
  30.0 83.3 %collective-permute-start.4 = (bf16[2,832,512]{2,1,0:T(8,128)(2,1)S(1)}, bf16[2,832,512]{2,1,0:T(8,128)(2,1)}, u32[]{:S(2)}, u32[]{:S(2)}) collective-permute-start(bf16[2,832,512]{2,1,0:T(8,128)(2,1)S(1)} %maximum_select_fusion.2), channel_id=1, source_target_pairs={{0,256},{16,272},{32,288},{48,304},{64,320},{80,336},{96,352},{112... | collective-permute-start | bytes 5111816 | tf_op jit(solution)/shard_map/ppermute | solution.py:16
  39.9 7.1 %collective-permute-start = (bf16[64,1664]{1,0:T(8,128)(2,1)S(1)}, bf16[64,1664]{1,0:T(8,128)(2,1)S(1)}, u32[]{:S(2)}, u32[]{:S(2)}) collective-permute-start(bf16[64,1664]{1,0:T(8,128)(2,1)S(1)} %copy-done.4), channel_id=1, source_target_pairs={{0,16},{16,0},{32,48},{48,32},{64,80},{80,64},{96,112},{112,96},{1... | collective-permute-start | bytes 638984 | tf_op jit(solution)/shard_map/ppermute | solution.py:16
  47.1 22.6 %collective-permute-start.1 = (bf16[128,1664]{1,0:T(8,128)(2,1)S(1)}, bf16[128,1664]{1,0:T(8,128)(2,1)S(1)}, u32[]{:S(2)}, u32[]{:S(2)}) collective-permute-start(bf16[128,1664]{1,0:T(8,128)(2,1)S(1)} %maximum_select_fusion.4), channel_id=1, source_target_pairs={{0,32},{16,48},{32,0},{48,16},{64,96},{80,112},{96,64},{112,80},{1... | collective-permute-start | bytes 1277960 | tf_op jit(solution)/shard_map/ppermute | solution.py:16
  70.8 46.4 %collective-permute-start.2 = (bf16[256,1664]{1,0:T(8,128)(2,1)}, bf16[256,1664]{1,0:T(8,128)(2,1)}, u32[]{:S(2)}, u32[]{:S(2)}) collective-permute-start(bf16[256,1664]{1,0:T(8,128)(2,1)} %maximum_select_fusion.3), channel_id=1, source_target_pairs={{0,64},{16,80},{32,96},{48,112},{64,0},{80,16},{96,32},{112,48},{1... | collective-permute-start | bytes 2555912 | tf_op jit(solution)/shard_map/ppermute | solution.py:16
  138.3 2.5 copy-start.1
  138.3 2.5 copy-start.3
  140.8 2.1 copy-start.7
  357.3 36.2 %collective-permute-start.5 = (bf16[256,1664]{1,0:T(8,128)(2,1)S(1)}, bf16[256,1664]{1,0:T(8,128)(2,1)S(1)}, u32[]{:S(2)}, u32[]{:S(2)}) collective-permute-start(bf16[256,1664]{1,0:T(8,128)(2,1)S(1)} %select_convert_fusion), channel_id=1, source_target_pairs={{0,64},{16,80},{32,96},{48,112},{64,0},{80,16},{96,32},{112,48},{1... | collective-permute-start | bytes 2555912 | tf_op jit(solution)/shard_map/ppermute | solution.py:16
  393.8 33.9 %copy-start.2 = (bf16[16,64,4,128]{3,1,2,0:T(8,128)(2,1)S(1)}, bf16[16,64,4,128]{3,1,2,0:T(8,128)(2,1)}, u32[]{:S(2)}) copy-start(bf16[16,64,4,128]{3,1,2,0:T(8,128)(2,1)} %gather_fusion) | copy-start | bytes 3145732
  393.8 33.9 %copy-start.8 = (f32[16,4,64,64]{3,2,1,0:T(8,128)S(1)}, f32[16,4,64,64]{3,2,1,0:T(8,128)}, u32[]{:S(2)}) copy-start(f32[16,4,64,64]{3,2,1,0:T(8,128)} %copy-done.7) | copy-start | bytes 3145732
  393.8 31.8 %collective-permute-start.6 = (bf16[128,1664]{1,0:T(8,128)(2,1)S(1)}, bf16[128,1664]{1,0:T(8,128)(2,1)S(1)}, u32[]{:S(2)}, u32[]{:S(2)}) collective-permute-start(bf16[128,1664]{1,0:T(8,128)(2,1)S(1)} %select_convert_fusion.1), channel_id=1, source_target_pairs={{0,32},{16,48},{32,0},{48,16},{64,96},{80,112},{96,64},{112,80},{1... | collective-permute-start | bytes 1277960 | tf_op jit(solution)/shard_map/ppermute | solution.py:16
  425.7 7.5 %collective-permute-start.7 = (bf16[64,1664]{1,0:T(8,128)(2,1)S(1)}, bf16[64,1664]{1,0:T(8,128)(2,1)S(1)}, u32[]{:S(2)}, u32[]{:S(2)}) collective-permute-start(bf16[64,1664]{1,0:T(8,128)(2,1)S(1)} %select_convert_fusion.2), channel_id=1, source_target_pairs={{0,16},{16,0},{32,48},{48,32},{64,80},{80,64},{96,112},{112,96},{1... | collective-permute-start | bytes 638984 | tf_op jit(solution)/shard_map/ppermute | solution.py:16
Sparse Core Ops, SparseCore 0:
  158.7 196.7 all-reduce.1
where the time goes:
time: 442 us; the launch traced here: 441 us
  waiting for transfers between devices  312 us (71%)
  starting transfers between devices  52.9 us (12%)
  matrix products  28.4 us (6%)
  local copies, waits for them, and re-layouts  20 us (5%)
  between operations  15.2 us (3%)
  other arithmetic  12.7 us (3%)
    psum x1, waiting for transfers between devices, shards(): summed = lax.psum(term.astype(jnp.bfloat16), 'tensor').astype(jnp.float32)  197 us
    ppermute x8, waiting for transfers between devices, from_partner(): return lax.ppermute(value, axis, pairs)  115 us
    ppermute x8, starting transfers between devices, from_partner(): return lax.ppermute(value, axis, pairs)  52.8 us
  transfers between devices with their start and end apart: 9, of which 8 were waited for; matrix products, arithmetic and copies ran while one was open for 3% of the time, Pallas kernels for 0%

commit v1 on v0

--- a/solution.py
+++ b/solution.py
@@ -127,7 +127,9 @@
         key_rows, value_rows, queries[0], gate_value, out_grad[0], own_visible, heads
     )
     term = back_product(key_grad, w_key) + back_product(value_grad, w_value)
-    summed = lax.psum(term.astype(jnp.bfloat16), "tensor").astype(jnp.float32)
+    summed = jnp.sum(lax.all_gather(term.astype(jnp.bfloat16), "tensor"), axis=0).astype(
+        jnp.float32
+    )
     owned = reduce_first(summed, position, layer_bits).astype(jnp.bfloat16)
     return (attended[None], owned)
 

time: 442 us -> 522 us (1.18)
  waiting for transfers between devices: 312 us -> 384 us
  other arithmetic: 12.7 us -> 21.1 us
    all_gather x0 -> x1, waiting for transfers between devices: none -> 269 us  [shards(): lax.all_gather(term.astype(jnp.bfloat16), 'tensor')]
    psum x1 -> x0, waiting for transfers between devices: 197 us -> none  [shards(): summed = lax.psum(term.astype(jnp.bfloat16), 'tensor').astype(jnp.float32)]
    reduce_sum x0 -> x1, other arithmetic: none -> 9.95 us  [shards(): jnp.sum(lax.all_gather(term.astype(jnp.bfloat16), 'tensor'), axis=0)]
where the time goes in v1:
time: 522 us
  waiting for transfers between devices  384 us (74%)
  starting transfers between devices  52.7 us (10%)
  matrix products  28.6 us (5%)
  other arithmetic  21.1 us (4%)
  local copies, waits for them, and re-layouts  20 us (4%)
  between operations  15.2 us (3%)
    all_gather x1, waiting for transfers between devices, shards(): lax.all_gather(term.astype(jnp.bfloat16), 'tensor')  269 us
    ppermute x8, waiting for transfers between devices, from_partner(): return lax.ppermute(value, axis, pairs)  115 us
    ppermute x8, starting transfers between devices, from_partner(): return lax.ppermute(value, axis, pairs)  52.7 us
  transfers between devices with their start and end apart: 9, of which 8 were waited for; matrix products, arithmetic and copies ran while one was open for 3% of the time, Pallas kernels for 0%

profile of v1, /device:TPU:1, one launch (start us, length us, event | category | flops | bytes accessed | tf_op | source)
XLA Modules:
  0.0 521.6 jit_solution(10425979873833213354)
XLA Ops:
  7.2 1.2 pad_maximum_fusion
  8.5 5.0 collective-permute-start.3
  13.5 14.5 %collective-permute-done.3 = bf16[2,416,512]{2,1,0:T(8,128)(2,1)S(1)} collective-permute-done((bf16[2,416,512]{2,1,0:T(8,128)(2,1)S(1)}, bf16[2,416,512]{2,1,0:T(8,128)(2,1)S(1)}, u32[]{:S(2)}, u32[]{:S(2)}) %collective-permute-start.3) | collective-permute-done | bytes 852000 | tf_op jit(solution)/shard_map/ppermute | solution.py:16
  28.0 1.9 maximum_select_fusion.2
  29.9 9.9 %collective-permute-start.4 = (bf16[2,832,512]{2,1,0:T(8,128)(2,1)S(1)}, bf16[2,832,512]{2,1,0:T(8,128)(2,1)}, u32[]{:S(2)}, u32[]{:S(2)}) collective-permute-start(bf16[2,832,512]{2,1,0:T(8,128)(2,1)S(1)} %maximum_select_fusion.2), channel_id=1, source_target_pairs={{0,256},{16,272},{32,288},{48,304},{64,320},{80,336},{96,352},{112... | collective-permute-start | bytes 5111816 | tf_op jit(solution)/shard_map/ppermute | solution.py:16
  39.8 3.2 collective-permute-start
  43.1 0.6 dynamic_slice.8
  44.7 2.3 collective-permute-done
  47.0 4.2 collective-permute-start.1
  51.3 1.4 multiply_convert_fusion.1
  52.7 16.9 %collective-permute-done.1 = bf16[128,1664]{1,0:T(8,128)(2,1)S(1)} collective-permute-done((bf16[128,1664]{1,0:T(8,128)(2,1)S(1)}, bf16[128,1664]{1,0:T(8,128)(2,1)S(1)}, u32[]{:S(2)}, u32[]{:S(2)}) %collective-permute-start.1) | collective-permute-done | bytes 426016 | tf_op jit(solution)/shard_map/ppermute | solution.py:16
  69.6 1.1 maximum_select_fusion.3
  70.7 8.4 %collective-permute-start.2 = (bf16[256,1664]{1,0:T(8,128)(2,1)}, bf16[256,1664]{1,0:T(8,128)(2,1)}, u32[]{:S(2)}, u32[]{:S(2)}) collective-permute-start(bf16[256,1664]{1,0:T(8,128)(2,1)} %maximum_select_fusion.3), channel_id=1, source_target_pairs={{0,64},{16,80},{32,96},{48,112},{64,0},{80,16},{96,32},{112,48},{1... | collective-permute-start | bytes 2555912 | tf_op jit(solution)/shard_map/ppermute | solution.py:16
  79.2 2.1 reshape_squeeze.3
  81.3 1.1 convert_element_type.91
  82.5 30.7 %collective-permute-done.4 = bf16[2,832,512]{2,1,0:T(8,128)(2,1)} collective-permute-done((bf16[2,832,512]{2,1,0:T(8,128)(2,1)S(1)}, bf16[2,832,512]{2,1,0:T(8,128)(2,1)}, u32[]{:S(2)}, u32[]{:S(2)}) %collective-permute-start.4) | collective-permute-done | bytes 1703968 | tf_op jit(solution)/shard_map/ppermute | solution.py:16
  113.2 3.9 maximum_select_fusion
  117.1 4.0 fusion.19
  121.0 2.0 reshape.62
  123.0 2.0 copy.13
  125.0 4.0 fusion.18
  128.9 2.0 reshape.63
  130.9 2.0 copy.14
  132.9 2.7 gather_fusion
  135.6 2.7 gather_fusion.1
  138.3 2.5 bitcast_reduce_fusion
  140.8 2.1 fusion.32
  142.8 1.7 fusion.30
  144.5 6.2 %fusion.12 = bf16[16,4,64,128]{3,2,1,0:T(8,128)(2,1)} fusion(f32[16,4,64,64]{2,3,1,0:T(8,128)} %fusion.32, bf16[16,64,4,128]{3,2,1,0:T(4,128)(2,1)} %reshape_squeeze.3, f32[16,4,64,64]{3,2,1,0:T(8,128)} %copy-done.7, f32[16]{0:T(128)S(1)} %reshape.64, f32[16,4,64]{2,1,0:T(4,128)S(1)} %get-tuple-element.5), kind=kOutput, calls=%fused_computation.20 | convolution fusion | flops 69996608 | bytes 4210752 | tf_op jit(solution)/shard_map/bhqk,bqhd->bkhd/dot_general | solution.py:58
  150.7 2.0 fusion.23
  152.6 2.0 fusion.20
  154.6 0.2 copy.20
  155.0 1.2 fusion.14
  156.2 2.4 add_convert_fusion
  158.6 268.9 %all-gather.3.cloned.1.call-done = bf16[8192,1664]{1,0:T(8,128)(2,1)} async-done(((bf16[512,1664]{1,0:T(8,128)(2,1)}), bf16[8192,1664]{1,0:T(8,128)(2,1)}) %all-gather.3.cloned.1.call-update) | async-done | bytes 27262992 | tf_op jit(solution)/shard_map/all_gather | solution.py:130
  427.5 9.9 %reduce_sum.32 = bf16[512,1664]{1,0:T(8,128)(2,1)S(1)} reduce(bf16[16,512,1664]{2,1,0:T(8,128)(2,1)} %bitcast.64, bf16[]{:T(256)} %constant.133.clone.1), dimensions={0}, to_apply=%region_2.4 | reduce | flops 12779520 | bytes 28966914 | tf_op jit(solution)/shard_map/reduce_sum | solution.py:130
  437.5 0.2 convert_element_type.98
  437.9 7.1 %collective-permute-start.5 = (bf16[256,1664]{1,0:T(8,128)(2,1)S(1)}, bf16[256,1664]{1,0:T(8,128)(2,1)S(1)}, u32[]{:S(2)}, u32[]{:S(2)}) collective-permute-start(bf16[256,1664]{1,0:T(8,128)(2,1)S(1)} %select_convert_fusion), channel_id=1, source_target_pairs={{0,64},{16,80},{32,96},{48,112},{64,0},{80,16},{96,32},{112,48},{1... | collective-permute-start | bytes 2555912 | tf_op jit(solution)/shard_map/ppermute | solution.py:16
  445.0 29.2 %collective-permute-done.5 = bf16[256,1664]{1,0:T(8,128)(2,1)S(1)} collective-permute-done((bf16[256,1664]{1,0:T(8,128)(2,1)S(1)}, bf16[256,1664]{1,0:T(8,128)(2,1)S(1)}, u32[]{:S(2)}, u32[]{:S(2)}) %collective-permute-start.5) | collective-permute-done | bytes 852000 | tf_op jit(solution)/shard_map/ppermute | solution.py:16
  474.2 0.2 convert_add_fusion
  474.5 13.0 %collective-permute-start.6 = (bf16[128,1664]{1,0:T(8,128)(2,1)S(1)}, bf16[128,1664]{1,0:T(8,128)(2,1)S(1)}, u32[]{:S(2)}, u32[]{:S(2)}) collective-permute-start(bf16[128,1664]{1,0:T(8,128)(2,1)S(1)} %select_convert_fusion.1), channel_id=1, source_target_pairs={{0,32},{16,48},{32,0},{48,16},{64,96},{80,112},{96,64},{112,80},{1... | collective-permute-start | bytes 1277960 | tf_op jit(solution)/shard_map/ppermute | solution.py:16
  487.4 18.8 %collective-permute-done.6 = bf16[128,1664]{1,0:T(8,128)(2,1)S(1)} collective-permute-done((bf16[128,1664]{1,0:T(8,128)(2,1)S(1)}, bf16[128,1664]{1,0:T(8,128)(2,1)S(1)}, u32[]{:S(2)}, u32[]{:S(2)}) %collective-permute-start.6) | collective-permute-done | bytes 426016 | tf_op jit(solution)/shard_map/ppermute | solution.py:16
  506.4 1.9 collective-permute-start.7
  508.4 0.9 fusion.17
  509.3 0.9 copy.18
  510.1 1.2 broadcast_in_dim_reshape.4
  511.4 2.7 collective-permute-done.7
  514.0 0.7 add_convert_fusion.1
  (37 shorter events, 1.1 us)
Async XLA Ops:
  7.2 420.4 %all-gather.3.cloned.1.call-start = ((), (), s32[]{:S(2)}) async-start(), calls=%async_computation | async-start | bytes 28966912 | tf_op jit(solution)/shard_map/all_gather | solution.py:130
  8.4 31.4 %copy-start.4 = (bf16[64,1664]{1,0:T(8,128)(2,1)S(1)}, bf16[64,1664]{1,0:T(8,128)(2,1)}, u32[]{:S(2)}) copy-start(bf16[64,1664]{1,0:T(8,128)(2,1)} %param.9) | copy-start | bytes 638980
  8.4 34.7 %copy-start.6 = (f32[8]{0:T(128)S(1)}, f32[8]{0:T(128)}, u32[]{:S(2)}) copy-start(f32[8]{0:T(128)} %param.13) | copy-start | bytes 100
  8.5 36.1 %copy-start.5 = (s32[4,4,4]{2,1,0:T(4,128)S(1)}, s32[4,4,4]{2,1,0:T(4,128)}, u32[]{:S(2)}) copy-start(s32[4,4,4]{2,1,0:T(4,128)} %param.14) | copy-start | bytes 772
  8.5 19.5 %collective-permute-start.3 = (bf16[2,416,512]{2,1,0:T(8,128)(2,1)S(1)}, bf16[2,416,512]{2,1,0:T(8,128)(2,1)S(1)}, u32[]{:S(2)}, u32[]{:S(2)}) collective-permute-start(bf16[2,416,512]{2,1,0:T(8,128)(2,1)S(1)} %pad_maximum_fusion), channel_id=1, source_target_pairs={{0,128},{16,144},{32,160},{48,176},{64,192},{80,208},{96,224},{112... | collective-permute-start | bytes 2555912 | tf_op jit(solution)/shard_map/ppermute | solution.py:16
  29.8 40.8 %copy-start = (bf16[2,832,512]{2,1,0:T(8,128)(2,1)}, bf16[2,832,512]{2,1,0:T(8,128)(2,1)S(1)}, u32[]{:S(2)}) copy-start(bf16[2,832,512]{2,1,0:T(8,128)(2,1)S(1)} %maximum_select_fusion.2) | copy-start | bytes 5111812
  29.9 83.3 %collective-permute-start.4 = (bf16[2,832,512]{2,1,0:T(8,128)(2,1)S(1)}, bf16[2,832,512]{2,1,0:T(8,128)(2,1)}, u32[]{:S(2)}, u32[]{:S(2)}) collective-permute-start(bf16[2,832,512]{2,1,0:T(8,128)(2,1)S(1)} %maximum_select_fusion.2), channel_id=1, source_target_pairs={{0,256},{16,272},{32,288},{48,304},{64,320},{80,336},{96,352},{112... | collective-permute-start | bytes 5111816 | tf_op jit(solution)/shard_map/ppermute | solution.py:16
  39.8 7.1 %collective-permute-start = (bf16[64,1664]{1,0:T(8,128)(2,1)S(1)}, bf16[64,1664]{1,0:T(8,128)(2,1)S(1)}, u32[]{:S(2)}, u32[]{:S(2)}) collective-permute-start(bf16[64,1664]{1,0:T(8,128)(2,1)S(1)} %copy-done.4), channel_id=1, source_target_pairs={{0,16},{16,0},{32,48},{48,32},{64,80},{80,64},{96,112},{112,96},{1... | collective-permute-start | bytes 638984 | tf_op jit(solution)/shard_map/ppermute | solution.py:16
  47.0 22.6 %collective-permute-start.1 = (bf16[128,1664]{1,0:T(8,128)(2,1)S(1)}, bf16[128,1664]{1,0:T(8,128)(2,1)S(1)}, u32[]{:S(2)}, u32[]{:S(2)}) collective-permute-start(bf16[128,1664]{1,0:T(8,128)(2,1)S(1)} %maximum_select_fusion.4), channel_id=1, source_target_pairs={{0,32},{16,48},{32,0},{48,16},{64,96},{80,112},{96,64},{112,80},{1... | collective-permute-start | bytes 1277960 | tf_op jit(solution)/shard_map/ppermute | solution.py:16
  70.7 46.4 %collective-permute-start.2 = (bf16[256,1664]{1,0:T(8,128)(2,1)}, bf16[256,1664]{1,0:T(8,128)(2,1)}, u32[]{:S(2)}, u32[]{:S(2)}) collective-permute-start(bf16[256,1664]{1,0:T(8,128)(2,1)} %maximum_select_fusion.3), channel_id=1, source_target_pairs={{0,64},{16,80},{32,96},{48,112},{64,0},{80,16},{96,32},{112,48},{1... | collective-permute-start | bytes 2555912 | tf_op jit(solution)/shard_map/ppermute | solution.py:16
  138.3 2.5 copy-start.1
  138.3 2.5 copy-start.3
  140.8 2.1 copy-start.7
  437.9 36.3 %collective-permute-start.5 = (bf16[256,1664]{1,0:T(8,128)(2,1)S(1)}, bf16[256,1664]{1,0:T(8,128)(2,1)S(1)}, u32[]{:S(2)}, u32[]{:S(2)}) collective-permute-start(bf16[256,1664]{1,0:T(8,128)(2,1)S(1)} %select_convert_fusion), channel_id=1, source_target_pairs={{0,64},{16,80},{32,96},{48,112},{64,0},{80,16},{96,32},{112,48},{1... | collective-permute-start | bytes 2555912 | tf_op jit(solution)/shard_map/ppermute | solution.py:16
  474.5 33.9 %copy-start.2 = (bf16[16,64,4,128]{3,1,2,0:T(8,128)(2,1)S(1)}, bf16[16,64,4,128]{3,1,2,0:T(8,128)(2,1)}, u32[]{:S(2)}) copy-start(bf16[16,64,4,128]{3,1,2,0:T(8,128)(2,1)} %gather_fusion) | copy-start | bytes 3145732
  474.5 33.9 %copy-start.8 = (f32[16,4,64,64]{3,2,1,0:T(8,128)S(1)}, f32[16,4,64,64]{3,2,1,0:T(8,128)}, u32[]{:S(2)}) copy-start(f32[16,4,64,64]{3,2,1,0:T(8,128)} %copy-done.7) | copy-start | bytes 3145732
  474.5 31.8 %collective-permute-start.6 = (bf16[128,1664]{1,0:T(8,128)(2,1)S(1)}, bf16[128,1664]{1,0:T(8,128)(2,1)S(1)}, u32[]{:S(2)}, u32[]{:S(2)}) collective-permute-start(bf16[128,1664]{1,0:T(8,128)(2,1)S(1)} %select_convert_fusion.1), channel_id=1, source_target_pairs={{0,32},{16,48},{32,0},{48,16},{64,96},{80,112},{96,64},{112,80},{1... | collective-permute-start | bytes 1277960 | tf_op jit(solution)/shard_map/ppermute | solution.py:16
  506.4 7.6 %collective-permute-start.7 = (bf16[64,1664]{1,0:T(8,128)(2,1)S(1)}, bf16[64,1664]{1,0:T(8,128)(2,1)S(1)}, u32[]{:S(2)}, u32[]{:S(2)}) collective-permute-start(bf16[64,1664]{1,0:T(8,128)(2,1)S(1)} %select_convert_fusion.2), channel_id=1, source_target_pairs={{0,16},{16,0},{32,48},{48,32},{64,80},{80,64},{96,112},{112,96},{1... | collective-permute-start | bytes 638984 | tf_op jit(solution)/shard_map/ppermute | solution.py:16
Sparse Core Ops, SparseCore 0:
  158.7 268.7 all-gather.2
